TPU v7x, 768 devices: a whole 4x8x12 slice. The times are simulated.
768 devices in a mesh: group: 64 (over y, x, core), member: 12 (over z).
Axes of the slice: x: 4, y: 8, z: 12, core: 2. Of those that a mesh axis runs over, the one named last changes fastest.
Arguments:
- state: bfloat16 [64, 12, 128, 9, 256], P('group', 'member'), may hold values from -6 to 6
- coef: bfloat16 [64, 12, 128, 256], P('group', 'member'), may hold values from 0.5 to 2
- new_group: int32 [64, 12, 128], P('group', 'member'), may hold values from -1 to 63, as said below
- face_lists: int32 [64, 12, 6, 128], P('group', 'member'), may hold values from -1 to 127
- lewis: float32 [9], replicated, may hold values from 0.3 to 3
Outputs:
- smoothed: float32 [64, 12, 128, 9, 256], P('group', 'member')
Inputs may be any that keep to these rules, and one draw needn't show every extreme that they name: -1 marks an old slot that holds no patch. A patch keeps its member index. At most 2 patches go from one device to one device, and at most 128 arrive at one device. Counts, offsets and slot numbers derived from new_group may cross devices in any integer encoding.
All inputs are finite; a program needn't handle non-finite values.
Results may differ from a plain program's by a relative error of at most 0.0003.
Values may be sent and summed in bfloat16 or wider, within the bound.
A program may use at most 128 MiB of HBM per device.

v0:
```python
import jax
import jax.numpy as jnp
from jax import lax
from jax.sharding import PartitionSpec as P

PX = 16
PY = 16
SWEEPS = 2


def with_halo(block, sides, width):
    for axis, dim in sides:
        count = lax.axis_size(axis)
        forward = [(i, i + 1) for i in range(count - 1)]
        backward = [(target, source) for source, target in forward]
        low = lax.ppermute(
            lax.slice_in_dim(block, block.shape[dim] - width, None, axis=dim), axis, forward
        )
        high = lax.ppermute(lax.slice_in_dim(block, 0, width, axis=dim), axis, backward)
        block = jnp.concatenate([low, block, high], axis=dim)
    return block


def prefix(part, axis, combine, identity):
    place = lax.axis_index(axis)
    gathered = lax.all_gather(part, axis)
    state = jnp.zeros_like(part) + jnp.asarray(identity, part.dtype)

    def one(lap, state):
        return combine(state, lax.dynamic_index_in_dim(gathered, lap, 0, False))

    return lax.fori_loop(0, place, one, state)


def pick_rows(field, index):
    taken = jnp.take(field, jnp.clip(index, 0, field.shape[0] - 1), axis=0)
    return jnp.where((index >= 0)[:, None, None], taken, 0.0)


def beside_all(field, lists, lower, upper):
    slots, kinds, count = field.shape
    span = PX * PY
    depth = count // span
    cell = jnp.arange(count, dtype=jnp.int32)
    xpos = cell % PX
    ypos = cell // PX % PY
    x_low_edge = jnp.repeat(pick_rows(field[..., PX - 1 :: PX], lists[0]), PX, axis=-1)
    x_high_edge = jnp.repeat(pick_rows(field[..., 0::PX], lists[1]), PX, axis=-1)
    x_low = jnp.where(xpos == 0, x_low_edge, jnp.roll(field, 1, -1))
    x_high = jnp.where(xpos == PX - 1, x_high_edge, jnp.roll(field, -1, -1))
    layered = field.reshape(slots, kinds, depth, span)
    top_rows = layered[..., (PY - 1) * PX :].reshape(slots, kinds, depth * PX)
    bottom_rows = layered[..., :PX].reshape(slots, kinds, depth * PX)

    def spread(rows):
        shaped = rows.reshape(slots, kinds, depth, 1, PX)
        return jnp.broadcast_to(shaped, (slots, kinds, depth, PY, PX)).reshape(slots, kinds, count)

    y_low = jnp.where(ypos == 0, spread(pick_rows(top_rows, lists[2])), jnp.roll(field, PX, -1))
    y_high = jnp.where(
        ypos == PY - 1, spread(pick_rows(bottom_rows, lists[3])), jnp.roll(field, -PX, -1)
    )
    z_low = jnp.concatenate([pick_rows(lower, lists[4]), field[..., : count - span]], -1)
    z_high = jnp.concatenate([field[..., span:], pick_rows(upper, lists[5])], -1)
    return (x_low, x_high, y_low, y_high, z_low, z_high)


def sweep(phi, rhs, weights, lists, lower, upper, lewis):
    near = beside_all(phi, lists, lower, upper)
    flow = weights[0] * near[0]
    total = weights[0]
    for face in range(1, 6):
        flow = flow + weights[face] * near[face]
        total = total + weights[face]
    factor = lewis[:, None]
    return (rhs + factor * flow) / (1.0 + factor * total)


def faces_of(field):
    return jnp.stack([field, field], 0)


def face_fill(stacked):
    return with_halo(stacked, (("member", 0),), 1)


def make_weights(cell_coef, lists, lower, upper):
    near = beside_all(cell_coef, lists, lower, upper)
    return tuple((0.5 * (cell_coef + item) for item in near))


def per_device(state, coef, new_group, face_lists, lewis):
    groups = lax.axis_size("group")
    old_state = state[0, 0]
    old_coef = coef[0, 0]
    dest = new_group[0, 0]
    lists = face_lists[0, 0]
    slots = old_state.shape[0]
    capacity = slots // groups
    valid = dest >= 0
    onehot = (dest[:, None] == jnp.arange(groups, dtype=jnp.int32)[None, :]).astype(jnp.int32)
    running = jnp.sum(jnp.cumsum(onehot, 0) * onehot, axis=1) - 1
    position = jnp.where(valid, dest * capacity + running, groups * capacity)
    counts = jnp.sum(onehot, axis=0)
    offsets = prefix(
        counts, "group", lambda earlier, later: earlier + later, jnp.zeros_like(counts)
    )
    chosen = jnp.sum(onehot * offsets[None, :], axis=1) + running
    labels = (
        jnp.full((groups * capacity,), slots, jnp.int32)
        .at[position]
        .set(chosen.astype(jnp.int32), mode="drop")
    )
    send_state = (
        jnp.zeros((groups * capacity,) + old_state.shape[1:], jnp.bfloat16)
        .at[position]
        .set(old_state, mode="drop")
    )
    send_coef = (
        jnp.zeros((groups * capacity,) + old_coef.shape[1:], jnp.bfloat16)
        .at[position]
        .set(old_coef, mode="drop")
    )
    got_state, got_coef, got_labels = (
        lax.all_to_all(send_state, "group", split_axis=0, concat_axis=0, tiled=True),
        lax.all_to_all(send_coef, "group", split_axis=0, concat_axis=0, tiled=True),
        lax.all_to_all(labels, "group", split_axis=0, concat_axis=0, tiled=True),
    )
    rhs = (
        jnp.zeros(old_state.shape, jnp.float32)
        .at[got_labels]
        .set(got_state.astype(jnp.float32), mode="drop")
    )
    cell_coef = (
        jnp.zeros(old_coef.shape, jnp.float32)
        .at[got_labels]
        .set(got_coef.astype(jnp.float32), mode="drop")[:, None, :]
    )
    weights = None
    coef_ghosts = with_halo(faces_of(cell_coef).astype(jnp.bfloat16), (("member", 0),), 1).astype(
        jnp.float32
    )
    weights = make_weights(cell_coef, lists, coef_ghosts[0], coef_ghosts[3])
    phi = rhs
    for step in range(SWEEPS):
        ghosts = face_fill(faces_of(phi))
        lower = ghosts[0]
        upper = ghosts[3]
        phi = sweep(phi, rhs, weights, lists, lower, upper, lewis)
    return phi[None, None]


def solution(mesh):
    return jax.shard_map(
        per_device,
        mesh=mesh,
        in_specs=(
            P("group", "member", None, None, None),
            P("group", "member", None, None),
            P("group", "member", None),
            P("group", "member", None, None),
            P(),
        ),
        out_specs=P("group", "member", None, None, None),
        check_vma=False,
    )
```

profile of v0, /device:TPU:6, one launch (start us, length us, event | category | flops | bytes accessed | tf_op | source)
XLA Modules:
  0.0 537.5 jit_solution(6205378377489541998)
XLA Ops:
  3.7 240.3 %all-reduce = s32[4096]{0:T(1024)S(1)} all-reduce(s32[4096]{0:T(1024)S(1)} %dynamic-update-slice), channel_id=2, replica_groups=mesh['group'=64,'member'=12] {'group'}, use_global_device_ids=true, to_apply=%add | all-reduce | flops 4096 | bytes 32768
  247.7 19.1 %all-to-all-start = ((s32[64,2,1]{1,2,0:T(1,128)}), s32[64,2,1]{1,2,0:T(1,128)S(1)}, u32[]{:S(2)}, u32[]{:S(2)}) async-start(s32[64,2,1]{1,2,0:T(1,128)} %bitcast.7), calls=%async_computation | async-start | bytes 65536 | tf_op jit(solution)/shard_map/all_to_all | solution.py:127
  272.8 15.3 %scatter_fusion = bf16[128,9,256]{2,1,0:T(8,128)(2,1)} fusion(bf16[128,9,256]{2,1,0:T(8,128)(2,1)} %broadcast_in_dim.310, s32[128]{0:T(128)S(1)} %fusion.63, bf16[128,9,256]{2,1,0:T(8,128)(2,1)S(1)} %copy.37), kind=kCustom, calls=%fused_computation.19 | custom fusion | bytes 1769984 | tf_op jit(solution)/shard_map/scatter | solution.py:117
  288.2 10.1 %all-to-all-start.2 = ((bf16[64,2,256]{2,1,0:T(2,128)(2,1)}), bf16[64,2,256]{2,1,0:T(2,128)(2,1)S(1)}, u32[]{:S(2)}, u32[]{:S(2)}) async-start(bf16[64,2,256]{2,1,0:T(2,128)(2,1)} %all_to_all.21), calls=%async_computation.2 | async-start | bytes 131072 | tf_op jit(solution)/shard_map/all_to_all | solution.py:126
  299.6 6.7 %all-to-all-done.2 = bf16[64,2,256]{2,1,0:T(2,128)(2,1)S(1)} async-done(((bf16[64,2,256]{2,1,0:T(2,128)(2,1)}), bf16[64,2,256]{2,1,0:T(2,128)(2,1)S(1)}, u32[]{:S(2)}, u32[]{:S(2)}) %all-to-all-start.2) | async-done | bytes 65568 | tf_op jit(solution)/shard_map/all_to_all | solution.py:126
  306.4 6.5 %all-to-all-start.1 = ((bf16[128,9,256]{2,1,0:T(8,128)(2,1)}), bf16[128,9,256]{2,1,0:T(8,128)(2,1)S(1)}, u32[]{:S(2)}, u32[]{:S(2)}) async-start(bf16[128,9,256]{2,1,0:T(8,128)(2,1)} %scatter_fusion), calls=%async_computation.1 | async-start | bytes 2097152 | tf_op jit(solution)/shard_map/all_to_all | solution.py:125
  315.3 4.7 collective-permute-start
  328.5 13.3 %all-to-all-done.1 = bf16[128,9,256]{2,1,0:T(8,128)(2,1)S(1)} async-done(((bf16[128,9,256]{2,1,0:T(8,128)(2,1)}), bf16[128,9,256]{2,1,0:T(8,128)(2,1)S(1)}, u32[]{:S(2)}, u32[]{:S(2)}) %all-to-all-start.1) | async-done | bytes 589856 | tf_op jit(solution)/shard_map/all_to_all | solution.py:125
  343.7 12.0 %scatter_fusion.1 = f32[128,9,256]{2,1,0:T(8,128)S(1)} fusion(f32[128,9,256]{2,1,0:T(8,128)S(1)} %broadcast_in_dim.308, s32[128]{0:T(128)S(1)} %fusion.62, f32[128,9,256]{2,1,0:T(8,128)} %convert_element_type.40), kind=kCustom, calls=%fused_computation.20 | custom fusion | bytes 3539456 | tf_op jit(solution)/shard_map/scatter | solution.py:132
  355.7 7.0 %slice.174 = f32[128,9,16]{2,1,0:T(8,128)S(1)} slice(f32[128,9,256]{2,1,0:T(8,128)S(1)} %scatter_fusion.1), slice={[0:128:1], [0:9:1], [15:256:16]} | slice | bytes 147456 | tf_op jit(solution)/shard_map/slice | solution.py:47
  364.3 7.4 %slice.181 = f32[128,9,16]{2,1,0:T(8,128)} slice(f32[128,9,256]{2,1,0:T(8,128)S(1)} %scatter_fusion.1), slice={[0:128:1], [0:9:1], [0:256:16]} | slice | bytes 147456 | tf_op jit(solution)/shard_map/slice | solution.py:48
  374.7 5.6 %collective-permute-start.2 = (f32[1,128,9,256]{3,1,2,0:T(8,128)}, f32[1,128,9,256]{3,1,2,0:T(8,128)}, u32[]{:S(2)}, u32[]{:S(2)}) collective-permute-start(f32[1,128,9,256]{3,1,2,0:T(8,128)} %copy.56), channel_id=1, source_target_pairs={{0,1},{1,2},{2,3},{3,4},{4,5},{5,6},{6,7},{7,8},{8,9},{9,10},{10,1... | collective-permute-start | bytes 3538952 | tf_op jit(solution)/shard_map/ppermute | solution.py:16
  382.0 2.6 select_select_fusion.11
  386.5 2.6 select_select_fusion.10
  390.8 1.9 gather_fusion.5
  398.8 2.0 copy.42
  402.3 2.0 copy.47
  405.8 1.9 copy.51
  409.3 1.9 copy.55
  412.9 2.7 fusion.78
  415.6 2.7 fusion.76
  418.3 3.4 copy.79
  421.6 3.8 gather_fusion.11
  425.4 3.4 copy.80
  428.8 3.8 gather_fusion.9
  432.7 10.2 %fusion.8 = f32[128,9,256]{2,1,0:T(8,128)S(1)} fusion(f32[128,9,256]{2,1,0:T(8,128)S(1)} %scatter_fusion.1, f32[128,9,256]{2,1,0:T(8,128)} %copy.42, f32[128,9,255]{2,1,0:T(8,128)} %get-tuple-element.77, f32[128,9,1]{2,1,0:T(8,128)} %get-tuple-element.79, f32[128,9,256]{2,1,0:T(8,128)} %copy.47, f32[128,9,1]{2,1,0:T(8,128)S(1)} %copy-done.6, ...), kind=kLoop, calls=%fused_computation.33 | loop fusion | flops 8257536 | bytes 15074852 | tf_op jit(solution)/shard_map/div | solution.py:76
  447.2 5.6 %collective-permute-start.4 = (f32[1,128,9,256]{3,1,2,0:T(8,128)}, f32[1,128,9,256]{3,1,2,0:T(8,128)}, u32[]{:S(2)}, u32[]{:S(2)}) collective-permute-start(f32[1,128,9,256]{3,1,2,0:T(8,128)} %copy.68), channel_id=1, source_target_pairs={{0,1},{1,2},{2,3},{3,4},{4,5},{5,6},{6,7},{7,8},{8,9},{9,10},{10,1... | collective-permute-start | bytes 3538952 | tf_op jit(solution)/shard_map/ppermute | solution.py:16
  452.8 7.6 %slice.206 = f32[128,9,16]{2,1,0:T(8,128)} slice(f32[128,9,256]{2,1,0:T(8,128)} %copy-done.2), slice={[0:128:1], [0:9:1], [0:256:16]} | slice | bytes 147456 | tf_op jit(solution)/shard_map/slice | solution.py:48
  460.4 6.9 %slice.203 = f32[128,9,16]{2,1,0:T(8,128)S(1)} slice(f32[128,9,256]{2,1,0:T(8,128)} %copy-done.2), slice={[0:128:1], [0:9:1], [15:256:16]} | slice | bytes 147456 | tf_op jit(solution)/shard_map/slice | solution.py:47
  467.4 3.2 slice_bitcast_fusion.1
  470.6 3.0 gather_fusion.15
  473.6 3.0 gather_fusion.14
  476.5 3.0 gather_fusion.13
  479.6 1.9 gather_fusion.12
  481.6 3.8 select_select_fusion.4
  485.5 2.3 select_select_fusion.6
  489.9 2.0 copy.67
  493.4 1.9 copy.65
  496.9 2.0 copy.63
  500.4 2.0 copy.61
  502.4 3.3 fusion.72
  505.7 2.7 fusion.75
  508.5 2.8 fusion.73
  511.2 3.4 copy.77
  514.6 3.8 gather_fusion.17
  518.4 3.4 copy.78
  521.8 3.8 gather_fusion.16
  525.7 10.1 %fusion.28 = f32[1,1,128,9,256]{4,3,2,1,0:T(8,128)S(1)} fusion(f32[128,9,256]{2,1,0:T(8,128)S(1)} %scatter_fusion.1, f32[128,9,256]{2,1,0:T(8,128)} %gather_fusion.17, f32[128,9,256]{2,1,0:T(8,128)} %gather_fusion.16, f32[128,9,256]{2,1,0:T(8,128)} %copy.67, f32[128,9,16]{2,1,0:T(8,128)} %get-tuple-element.65, f32[128,9,240]{2,1,0:T(8,128)} %get-tuple-element.67, ...), kind=kLoop, calls=%fused_computation.69 | loop fusion | flops 8257536 | bytes 15074852 | tf_op jit(solution)/shard_map/broadcast_in_dim | solution.py:150
  (224 shorter events, 61.5 us)
Async XLA Ops:
  0.0 270.1 %copy-start = (bf16[1,1,128,256]{3,2,1,0:T(8,128)(2,1)S(1)}, bf16[1,1,128,256]{3,2,1,0:T(8,128)(2,1)}, u32[]{:S(2)}) copy-start(bf16[1,1,128,256]{3,2,1,0:T(8,128)(2,1)} %param.16) | copy-start | bytes 196612
  247.7 40.5 %all-to-all-start = ((s32[64,2,1]{1,2,0:T(1,128)}), s32[64,2,1]{1,2,0:T(1,128)S(1)}, u32[]{:S(2)}, u32[]{:S(2)}) async-start(s32[64,2,1]{1,2,0:T(1,128)} %bitcast.7), calls=%async_computation | async-start | bytes 65536 | tf_op jit(solution)/shard_map/all_to_all | solution.py:127
  267.6 114.5 %copy-start.18 = (pred[128]{0:T(512)(128)(4,1)}, pred[128]{0:T(512)(128)(4,1)S(1)}, u32[]{:S(2)}) copy-start(pred[128]{0:T(512)(128)(4,1)S(1)} %get-tuple-element.102) | copy-start | bytes 388
  267.6 118.9 %copy-start.20 = (pred[128]{0:T(512)(128)(4,1)}, pred[128]{0:T(512)(128)(4,1)S(1)}, u32[]{:S(2)}) copy-start(pred[128]{0:T(512)(128)(4,1)S(1)} %get-tuple-element.104) | copy-start | bytes 388
  267.6 125.1 %copy-start.26 = (pred[128]{0:T(512)(128)(4,1)}, pred[128]{0:T(512)(128)(4,1)S(1)}, u32[]{:S(2)}) copy-start(pred[128]{0:T(512)(128)(4,1)S(1)} %get-tuple-element.106) | copy-start | bytes 388
  267.6 128.3 %copy-start.28 = (pred[128]{0:T(512)(128)(4,1)}, pred[128]{0:T(512)(128)(4,1)S(1)}, u32[]{:S(2)}) copy-start(pred[128]{0:T(512)(128)(4,1)S(1)} %get-tuple-element.108) | copy-start | bytes 388
  268.3 59.0 %copy-start.12 = (pred[128]{0:T(512)(128)(4,1)}, pred[128]{0:T(512)(128)(4,1)S(1)}, u32[]{:S(2)}) copy-start(pred[128]{0:T(512)(128)(4,1)S(1)} %get-tuple-element.96) | copy-start | bytes 388
  268.4 59.0 %copy-start.15 = (pred[128]{0:T(512)(128)(4,1)}, pred[128]{0:T(512)(128)(4,1)S(1)}, u32[]{:S(2)}) copy-start(pred[128]{0:T(512)(128)(4,1)S(1)} %get-tuple-element.101) | copy-start | bytes 388
  268.4 113.7 %copy-start.24 = (pred[128]{0:T(512)(128)(4,1)}, pred[128]{0:T(512)(128)(4,1)S(1)}, u32[]{:S(2)}) copy-start(pred[128]{0:T(512)(128)(4,1)S(1)} %get-tuple-element.100) | copy-start | bytes 388
  268.4 118.1 %copy-start.22 = (pred[128]{0:T(512)(128)(4,1)}, pred[128]{0:T(512)(128)(4,1)S(1)}, u32[]{:S(2)}) copy-start(pred[128]{0:T(512)(128)(4,1)S(1)} %get-tuple-element.99) | copy-start | bytes 388
  268.4 124.3 %copy-start.32 = (pred[128]{0:T(512)(128)(4,1)}, pred[128]{0:T(512)(128)(4,1)S(1)}, u32[]{:S(2)}) copy-start(pred[128]{0:T(512)(128)(4,1)S(1)} %get-tuple-element.98) | copy-start | bytes 388
  268.4 127.5 %copy-start.30 = (pred[128]{0:T(512)(128)(4,1)}, pred[128]{0:T(512)(128)(4,1)S(1)}, u32[]{:S(2)}) copy-start(pred[128]{0:T(512)(128)(4,1)S(1)} %get-tuple-element.97) | copy-start | bytes 388
  268.4 58.9 %copy-start.40 = (pred[256]{0:T(512)(128)(4,1)}, pred[256]{0:T(512)(128)(4,1)S(1)}, u32[]{:S(2)}) copy-start(pred[256]{0:T(512)(128)(4,1)S(1)} %broadcast_compare_fusion.3) | copy-start | bytes 772
  268.4 58.9 %copy-start.43 = (pred[256]{0:T(512)(128)(4,1)}, pred[256]{0:T(512)(128)(4,1)S(1)}, u32[]{:S(2)}) copy-start(pred[256]{0:T(512)(128)(4,1)S(1)} %broadcast_compare_fusion.1) | copy-start | bytes 772
  268.5 58.9 %copy-start.46 = (pred[256]{0:T(512)(128)(4,1)}, pred[256]{0:T(512)(128)(4,1)S(1)}, u32[]{:S(2)}) copy-start(pred[256]{0:T(512)(128)(4,1)S(1)} %broadcast_compare_fusion) | copy-start | bytes 772
  268.5 111.8 %copy-start.36 = (s32[1024]{0:T(1024)}, s32[1024]{0:T(1024)S(1)}, u32[]{:S(2)}) copy-start(s32[1024]{0:T(1024)S(1)} %pad_clamp_fusion.5) | copy-start | bytes 12292
  268.5 116.2 %copy-start.37 = (s32[1024]{0:T(1024)}, s32[1024]{0:T(1024)S(1)}, u32[]{:S(2)}) copy-start(s32[1024]{0:T(1024)S(1)} %pad_clamp_fusion.4) | copy-start | bytes 12292
  268.5 122.3 %copy-start.38 = (s32[1024]{0:T(1024)}, s32[1024]{0:T(1024)S(1)}, u32[]{:S(2)}) copy-start(s32[1024]{0:T(1024)S(1)} %pad_clamp_fusion.3) | copy-start | bytes 12292
  268.6 125.5 %copy-start.39 = (s32[1024]{0:T(1024)}, s32[1024]{0:T(1024)S(1)}, u32[]{:S(2)}) copy-start(s32[1024]{0:T(1024)S(1)} %pad_clamp_fusion.2) | copy-start | bytes 12292
  268.6 57.2 %copy-start.35 = (s32[1024]{0:T(1024)}, s32[1024]{0:T(1024)S(1)}, u32[]{:S(2)}) copy-start(s32[1024]{0:T(1024)S(1)} %pad_clamp_fusion) | copy-start | bytes 12292
  268.6 56.4 %copy-start.34 = (s32[1024]{0:T(1024)}, s32[1024]{0:T(1024)S(1)}, u32[]{:S(2)}) copy-start(s32[1024]{0:T(1024)S(1)} %pad_clamp_fusion.1) | copy-start | bytes 12292
  268.6 58.7 %copy-start.49 = (pred[256]{0:T(512)(128)(4,1)}, pred[256]{0:T(512)(128)(4,1)S(1)}, u32[]{:S(2)}) copy-start(pred[256]{0:T(512)(128)(4,1)S(1)} %broadcast_compare_fusion.2) | copy-start | bytes 772
  288.2 18.2 %all-to-all-start.2 = ((bf16[64,2,256]{2,1,0:T(2,128)(2,1)}), bf16[64,2,256]{2,1,0:T(2,128)(2,1)S(1)}, u32[]{:S(2)}, u32[]{:S(2)}) async-start(bf16[64,2,256]{2,1,0:T(2,128)(2,1)} %all_to_all.21), calls=%async_computation.2 | async-start | bytes 131072 | tf_op jit(solution)/shard_map/all_to_all | solution.py:126
  306.4 35.5 %all-to-all-start.1 = ((bf16[128,9,256]{2,1,0:T(8,128)(2,1)}), bf16[128,9,256]{2,1,0:T(8,128)(2,1)S(1)}, u32[]{:S(2)}, u32[]{:S(2)}) async-start(bf16[128,9,256]{2,1,0:T(8,128)(2,1)} %scatter_fusion), calls=%async_computation.1 | async-start | bytes 2097152 | tf_op jit(solution)/shard_map/all_to_all | solution.py:125
  314.0 11.0 %collective-permute-start.1 = (bf16[1,128,1,256]{3,1,0,2:T(8,128)(2,1)S(1)}, bf16[1,128,1,256]{3,1,0,2:T(8,128)(2,1)S(1)}, u32[]{:S(2)}, u32[]{:S(2)}) collective-permute-start(bf16[1,128,1,256]{3,1,0,2:T(8,128)(2,1)S(1)} %get-tuple-element.95), channel_id=1, source_target_pairs={{1,0},{2,1},{3,2},{4,3},{5,4},{6,5},{7,6},{8,7},{9,8},{10,9},{11,1... | collective-permute-start | bytes 196616 | tf_op jit(solution)/shard_map/ppermute | solution.py:19
  315.3 9.7 %collective-permute-start = (bf16[1,128,1,256]{3,1,0,2:T(8,128)(2,1)S(1)}, bf16[1,128,1,256]{3,1,0,2:T(8,128)(2,1)S(1)}, u32[]{:S(2)}, u32[]{:S(2)}) collective-permute-start(bf16[1,128,1,256]{3,1,0,2:T(8,128)(2,1)S(1)} %get-tuple-element.95), channel_id=1, source_target_pairs={{0,1},{1,2},{2,3},{3,4},{4,5},{5,6},{6,7},{7,8},{8,9},{9,10},{10,1... | collective-permute-start | bytes 196616 | tf_op jit(solution)/shard_map/ppermute | solution.py:16
  373.4 44.8 %collective-permute-start.3 = (f32[1,128,9,256]{3,1,2,0:T(8,128)}, f32[1,128,9,256]{3,1,2,0:T(8,128)}, u32[]{:S(2)}, u32[]{:S(2)}) collective-permute-start(f32[1,128,9,256]{3,1,2,0:T(8,128)} %copy.56), channel_id=1, source_target_pairs={{1,0},{2,1},{3,2},{4,3},{5,4},{6,5},{7,6},{8,7},{9,8},{10,9},{11,1... | collective-permute-start | bytes 3538952 | tf_op jit(solution)/shard_map/ppermute | solution.py:19
  374.7 50.7 %collective-permute-start.2 = (f32[1,128,9,256]{3,1,2,0:T(8,128)}, f32[1,128,9,256]{3,1,2,0:T(8,128)}, u32[]{:S(2)}, u32[]{:S(2)}) collective-permute-start(f32[1,128,9,256]{3,1,2,0:T(8,128)} %copy.56), channel_id=1, source_target_pairs={{0,1},{1,2},{2,3},{3,4},{4,5},{5,6},{6,7},{7,8},{8,9},{9,10},{10,1... | collective-permute-start | bytes 3538952 | tf_op jit(solution)/shard_map/ppermute | solution.py:16
  428.8 3.9 copy-start.41
  428.8 3.9 copy-start.44
  428.8 3.9 copy-start.47
  428.8 3.9 copy-start.50
  428.8 3.9 copy-start.52
  445.9 65.3 %collective-permute-start.5 = (f32[1,128,9,256]{3,1,2,0:T(8,128)}, f32[1,128,9,256]{3,1,2,0:T(8,128)}, u32[]{:S(2)}, u32[]{:S(2)}) collective-permute-start(f32[1,128,9,256]{3,1,2,0:T(8,128)} %copy.68), channel_id=1, source_target_pairs={{1,0},{2,1},{3,2},{4,3},{5,4},{6,5},{7,6},{8,7},{9,8},{10,9},{11,1... | collective-permute-start | bytes 3538952 | tf_op jit(solution)/shard_map/ppermute | solution.py:19
  447.2 71.2 %collective-permute-start.4 = (f32[1,128,9,256]{3,1,2,0:T(8,128)}, f32[1,128,9,256]{3,1,2,0:T(8,128)}, u32[]{:S(2)}, u32[]{:S(2)}) collective-permute-start(f32[1,128,9,256]{3,1,2,0:T(8,128)} %copy.68), channel_id=1, source_target_pairs={{0,1},{1,2},{2,3},{3,4},{4,5},{5,6},{6,7},{7,8},{8,9},{9,10},{10,1... | collective-permute-start | bytes 3538952 | tf_op jit(solution)/shard_map/ppermute | solution.py:16
  476.5 5.0 copy-start.27
  476.5 5.0 copy-start.29
  476.5 5.0 copy-start.31
  476.5 5.0 copy-start.33
  481.5 3.9 copy-start.8
  481.5 3.9 copy-start.9
  481.6 3.9 copy-start.19
  481.6 3.9 copy-start.21
  481.6 3.9 copy-start.23
  481.6 3.9 copy-start.25
  521.7 3.9 copy-start.42
  521.8 3.9 copy-start.45
  525.7 11.9 %copy-start.1 = (bf16[1,1,128,256]{3,2,1,0:T(8,128)(2,1)S(1)}, bf16[1,1,128,256]{3,2,1,0:T(8,128)(2,1)}, u32[]{:S(2)}) copy-start(bf16[1,1,128,256]{3,2,1,0:T(8,128)(2,1)} %param.16) | copy-start | bytes 196612
  (15 other events, 52.1 us)
where the time goes:
time: 540 us; the launch traced here: 538 us
  blocking collectives  240 us (44%)
  local copies, waits for them, and re-layouts  176 us (33%)
  starting transfers between devices  55.5 us (10%)
  other arithmetic  43.9 us (8%)
  waiting for transfers between devices  20.1 us (4%)
    unnamed x1, blocking collectives  240 us
    gather x18, local copies, waits for them, and re-layouts, pick_rows(): taken = jnp.take(field, jnp.clip(index, 0, field.shape[0] - 1), axis=0)  37.4 us
    all_to_all x1, starting transfers between devices, per_device(): lax.all_to_all(labels, 'group', split_axis=0, concat_axis=0, tiled=True)  19.1 us
    ppermute x3, starting transfers between devices, with_halo(): lax.ppermute(lax.slice_in_dim(block, block.shape[dim] - width, None, axis...  15.9 us
    slice x3, local copies, waits for them, and re-layouts, beside_all(): field[..., 0::PX]  15.4 us
    scatter x1, local copies, waits for them, and re-layouts, per_device(): send_state = jnp.zeros((groups * capacity,) + old_state.shape[1:], jnp.bf...  15.3 us
    select_n x8, other arithmetic, pick_rows(): return jnp.where((index >= 0)[:, None, None], taken, 0.0)  14.3 us
    slice x3, local copies, waits for them, and re-layouts, beside_all(): field[..., PX - 1::PX]  14.3 us
  transfers between devices with their start and end apart: 9, of which 2 were waited for; matrix products, arithmetic and copies ran while one was open for 26% of the time, Pallas kernels for 0%

commit v1 on v0

v1 whole, which is shorter than its diff:
```python
import functools
import math

import jax
import jax.numpy as jnp
from jax import lax
from jax.experimental import pallas as pl
from jax.experimental.pallas import tpu as pltpu
from jax.sharding import PartitionSpec as P

LANES = 128
EDGE = 16
MESH = pl.DeviceIdType.MESH
F32 = jnp.float32
BF16 = jnp.bfloat16


def dot(left, right):
    return jnp.dot(left, right, preferred_element_type=F32)


def iota(shape, dim):
    return lax.broadcasted_iota(jnp.int32, shape, dim)


def ones_where(mask):
    return jnp.where(mask, 1.0, 0.0).astype(BF16)


def beside(field, picked):
    rows = field.shape[0]
    low, high = field[:, :LANES], field[:, LANES:]
    lane = iota((rows, LANES), 1)
    xpos = lane % EDGE

    def turn(part, by):
        return pltpu.roll(part, by % LANES, 1)

    def halves(part):
        return part[:, :LANES], part[:, LANES:]

    def both(one, two):
        return jnp.concatenate([one, two], axis=1)

    a, b = halves(picked[0])
    x_low = both(
        jnp.where(xpos == 0, turn(a, 1 - EDGE), turn(low, 1)),
        jnp.where(xpos == 0, turn(b, 1 - EDGE), turn(high, 1)),
    )
    a, b = halves(picked[1])
    x_high = both(
        jnp.where(xpos == EDGE - 1, turn(a, EDGE - 1), turn(low, -1)),
        jnp.where(xpos == EDGE - 1, turn(b, EDGE - 1), turn(high, -1)),
    )
    first = lane < EDGE
    low_up, high_up = turn(low, EDGE), turn(high, EDGE)
    y_low = both(
        jnp.where(first, turn(picked[2][:, LANES:], EDGE), low_up),
        jnp.where(first, low_up, high_up),
    )
    last = lane >= LANES - EDGE
    low_down, high_down = turn(low, -EDGE), turn(high, -EDGE)
    y_high = both(
        jnp.where(last, high_down, low_down),
        jnp.where(last, turn(picked[3][:, :LANES], -EDGE), high_down),
    )
    return x_low, x_high, y_low, y_high


def split(value):
    head = value.astype(BF16)
    return head, (value - head.astype(F32)).astype(BF16)


def kernel(
    across, along, members, per,
    dest_ref, lists_ref, lewis_ref, coef_ref, state_ref, out_ref,
    send1, recv1, send2, arrived, below, above, kept, weight, total, pick1, pick2, ghost, ghost_low, ghost_high,
    s1, r1, s2, r2, sz, rz, sp, rp,
):
    species, slots, cells = state_ref.shape
    chunks = (species + 1) // per
    group, member = lax.axis_index("group"), lax.axis_index("member")
    yme, xme = group // across, group % across
    upper, lower = lax.rem(member + 1, members), lax.rem(member + members - 1, members)
    xrows, yrows = 2 * along, 2 * across

    def xpeer(step):
        return lax.rem(xme + step, across)

    def ypeer(step):
        return lax.rem(yme + step, along)

    barrier = pltpu.get_barrier_semaphore()
    for step in range(1, across):
        pl.semaphore_signal(barrier, inc=1, device_id=(yme * across + xpeer(step), member), device_id_type=MESH)
    for step in range(1, along):
        pl.semaphore_signal(barrier, inc=1, device_id=(ypeer(step) * across + xme, member), device_id_type=MESH)
    pl.semaphore_signal(barrier, inc=1, device_id=(group, upper), device_id_type=MESH)
    pl.semaphore_signal(barrier, inc=1, device_id=(group, lower), device_id_type=MESH)

    row = iota((slots, slots), 0)
    col = iota((slots, slots), 1)
    earlier = ones_where(row < col)

    target = (row % xrows) // 2 * across + row // xrows
    match = ones_where(dest_ref[...] == target)
    rank = dot(match, earlier).astype(jnp.int32)
    chosen = ones_where((match > 0) & (rank == row % 2))
    source = (row % yrows) // 2 * xrows + row // yrows * 2 + row % 2
    swap = ones_where(source == col)

    pl.semaphore_wait(barrier, across + along)

    def xcopy(chunk, step):
        rows = pl.ds(pl.multiple_of(xpeer(step) * xrows, xrows), xrows)
        mine = pl.ds(pl.multiple_of(xme * xrows, xrows), xrows)
        part = pl.ds(chunk * per, per)
        return pltpu.make_async_remote_copy(
            src_ref=send1.at[part, rows], dst_ref=recv1.at[part, mine],
            send_sem=s1.at[chunk, step], recv_sem=r1.at[chunk, step],
            device_id=(yme * across + xpeer(step), member), device_id_type=MESH,
        )

    def ycopy(chunk, step):
        rows = pl.ds(pl.multiple_of(ypeer(step) * yrows, yrows), yrows)
        mine = pl.ds(pl.multiple_of(yme * yrows, yrows), yrows)
        part = pl.ds(chunk * per, per)
        return pltpu.make_async_remote_copy(
            src_ref=send2.at[part, rows], dst_ref=arrived.at[part, mine],
            send_sem=s2.at[chunk, step], recv_sem=r2.at[chunk, step],
            device_id=(ypeer(step) * across + xme, member), device_id_type=MESH,
        )

    def zcopies(chunk):
        part = pl.ds(chunk * per, per)
        return [
            pltpu.make_async_remote_copy(
                src_ref=arrived.at[part], dst_ref=place.at[part],
                send_sem=sz.at[chunk, way], recv_sem=rz.at[chunk, way],
                device_id=(group, to), device_id_type=MESH,
            )
            for way, (place, to) in enumerate(((below, upper), (above, lower)))
        ]

    def gcopies(kind):
        return [
            pltpu.make_async_remote_copy(
                src_ref=ghost.at[kind], dst_ref=place.at[kind],
                send_sem=sp.at[kind, way], recv_sem=rp.at[kind, way],
                device_id=(group, to), device_id_type=MESH,
            )
            for way, (place, to) in enumerate(((ghost_low, upper), (ghost_high, lower)))
        ]

    def pack(chunk, first):
        for j in range(per):
            plane = chunk * per + j
            block = coef_ref[...] if first and j == 0 else state_ref[plane - 1]
            send1[plane] = dot(chosen, block).astype(BF16)
        part = pl.ds(chunk * per, per)
        mine = pl.ds(pl.multiple_of(xme * xrows, xrows), xrows)
        recv1[part, mine, :] = send1[part, mine, :]
        for step in range(1, across):
            xcopy(chunk, step).start()

    def turn(chunk):
        for step in range(1, across):
            xcopy(chunk, step).wait_recv()
        for j in range(per):
            plane = chunk * per + j
            send2[plane] = dot(swap, recv1[plane]).astype(BF16)
        part = pl.ds(chunk * per, per)
        mine = pl.ds(pl.multiple_of(yme * yrows, yrows), yrows)
        arrived[part, mine, :] = send2[part, mine, :]
        for step in range(1, along):
            ycopy(chunk, step).start()

    def forward(chunk):
        for step in range(1, along):
            ycopy(chunk, step).wait_recv()
        for copy in zcopies(chunk):
            copy.start()

    pack(0, True)
    pl.loop(1, chunks)(lambda chunk: pack(chunk, False))
    turn(0)

    @pl.loop(1, chunks)
    def _(chunk):
        turn(chunk)
        forward(chunk - 1)

    forward(chunks - 1)

    lists = lists_ref[...]
    for face in range(6):
        entry = lists[face : face + 1]
        if face == 4:
            entry = jnp.where(member == 0, -1, entry)
        if face == 5:
            entry = jnp.where(member == members - 1, -1, entry)
        hot = jnp.where(entry == row, 1.0, 0.0).T.astype(BF16)
        pick2[face] = hot

    def placing(field):
        lead = ones_where(iota((8, cells), 1) == 0)
        value = lax.dot_general(lead, field, (((1,), (1,)), ((), ())), preferred_element_type=F32)
        there = ones_where(value > 0.25)
        place = dot(there, earlier)[0:1].astype(jnp.int32)
        return ones_where((place == row) & (there[0:1] > 0))

    for copy in zcopies(0):
        copy.wait_recv()
    order = placing(arrived[0])
    pick1[0] = order
    for face in range(4):
        pick1[face + 1] = dot(pick2[face], order).astype(BF16)
    pick1[5] = dot(pick2[4], placing(below[0])).astype(BF16)
    pick1[6] = dot(pick2[5], placing(above[0])).astype(BF16)

    def first_near(plane):
        block = arrived[plane]
        field = dot(pick1[0], block)
        near = beside(field, [dot(pick1[face + 1], block) for face in range(4)])
        return field, near + (dot(pick1[5], below[plane]), dot(pick1[6], above[plane]))

    field, near = first_near(0)
    summed = None
    for face in range(6):
        part = 0.5 * (field + near[face])
        weight[face] = part
        summed = part if summed is None else summed + part
    total[...] = summed

    def relax(kind, rhs, near):
        flow = weight[0] * near[0]
        for face in range(1, 6):
            flow = flow + weight[face] * near[face]
        factor = lewis_ref[kind]
        return (rhs + factor * flow) / (1.0 + factor * total[...])

    @pl.loop(0, species)
    def _(kind):
        plane = kind + 1

        @pl.when(plane % per == 0)
        def _():
            for copy in zcopies(plane // per):
                copy.wait_recv()

        rhs, near = first_near(plane)
        kept[kind] = rhs.astype(BF16)
        phi = relax(kind, rhs, near)
        out_ref[kind] = phi
        head, tail = split(phi)
        ghost[kind, :slots, :] = head
        ghost[kind, slots:, :] = tail
        for copy in gcopies(kind):
            copy.start()

    @pl.loop(0, species)
    def _(kind):
        phi = out_ref[kind]
        pair = ghost[kind]
        near = beside(
            phi, [dot(jnp.concatenate([pick2[face], pick2[face]], axis=1), pair) for face in range(4)]
        )
        for copy in gcopies(kind):
            copy.wait_recv()
        ends = tuple(
            dot(jnp.concatenate([pick2[face], pick2[face]], axis=1), place[kind])
            for face, place in ((4, ghost_low), (5, ghost_high))
        )
        out_ref[kind] = relax(kind, kept[kind].astype(F32), near + ends)

    @pl.loop(0, chunks)
    def _(chunk):
        for step in range(1, across):
            xcopy(chunk, step).wait_send()
        for step in range(1, along):
            ycopy(chunk, step).wait_send()
        for copy in zcopies(chunk):
            copy.wait_send()

    @pl.loop(0, species)
    def _(kind):
        for copy in gcopies(kind):
            copy.wait_send()


def per_device(across, along, members, state, coef, new_group, face_lists, lewis):
    _, _, slots, species, cells = state.shape
    per = 2
    chunks = (species + 1) // per
    whole = pl.BlockSpec(memory_space=pltpu.VMEM)
    dma = pltpu.SemaphoreType.DMA
    planes = (species + 1, slots, cells)
    out = pl.pallas_call(
        functools.partial(kernel, across, along, members, per),
        out_shape=jax.ShapeDtypeStruct((species, slots, cells), F32),
        in_specs=[whole, whole, pl.BlockSpec(memory_space=pltpu.SMEM), whole, whole],
        out_specs=whole,
        scratch_shapes=[
            pltpu.VMEM(planes, BF16),
            pltpu.VMEM(planes, BF16),
            pltpu.VMEM(planes, BF16),
            pltpu.VMEM(planes, BF16),
            pltpu.VMEM(planes, BF16),
            pltpu.VMEM(planes, BF16),
            pltpu.VMEM((species, slots, cells), BF16),
            pltpu.VMEM((6, slots, cells), F32),
            pltpu.VMEM((slots, cells), F32),
            pltpu.VMEM((7, slots, slots), BF16),
            pltpu.VMEM((6, slots, slots), BF16),
            pltpu.VMEM((species, 2 * slots, cells), BF16),
            pltpu.VMEM((species, 2 * slots, cells), BF16),
            pltpu.VMEM((species, 2 * slots, cells), BF16),
            dma((chunks, across)),
            dma((chunks, across)),
            dma((chunks, along)),
            dma((chunks, along)),
            dma((chunks, 2)),
            dma((chunks, 2)),
            dma((species, 2)),
            dma((species, 2)),
        ],
        compiler_params=pltpu.CompilerParams(
            collective_id=0, has_side_effects=True, vmem_limit_bytes=40 * 2**20
        ),
        name="regrid_and_sweep",
    )(
        new_group[0],
        face_lists[0, 0],
        lewis,
        coef[0, 0],
        jnp.transpose(state[0, 0], (1, 0, 2)),
    )
    return jnp.transpose(out, (1, 0, 2))[None, None]


def solution(mesh):
    groups, members = mesh.shape["group"], mesh.shape["member"]
    across = math.isqrt(groups)
    return jax.shard_map(
        functools.partial(per_device, across, groups // across, members),
        mesh=mesh,
        in_specs=(
            P("group", "member", None, None, None),
            P("group", "member", None, None),
            P("group", "member", None),
            P("group", "member", None, None),
            P(),
        ),
        out_specs=P("group", "member", None, None, None),
        check_vma=False,
    )
```

time: 540 us -> 80.3 us (0.15)
  blocking collectives: 240 us -> 0 us
  local copies, waits for them, and re-layouts: 176 us -> 4.91 us
  Pallas kernels: 0 us -> 74.8 us
  starting transfers between devices: 55.5 us -> 0 us
  other arithmetic: 43.9 us -> 0 us
  waiting for transfers between devices: 20.1 us -> 0 us
    unnamed x1 -> x0, blocking collectives: 240 us -> none
    pallas_call x0 -> x1, Pallas kernels: none -> 74.8 us  [per_device(): pl.pallas_call(functools.partial(kernel, across, along, members, per), ou...]
    slice x14 -> x0, local copies, waits for them, and re-layouts: 48.9 us -> none  [the longest x3 15.4 us: beside_all(): field[..., 0::PX]]
    gather x18 -> x0, local copies, waits for them, and re-layouts: 37.4 us -> none  [pick_rows(): taken = jnp.take(field, jnp.clip(index, 0, field.shape[0] - 1), axis=0)]
    all_to_all x3 -> x0, starting transfers between devices: 35.8 us -> none  [the longest x1 19.1 us: per_device(): lax.all_to_all(labels, 'group', split_axis=0, concat_axis=0, tiled=True)]
    scatter x5 -> x0, local copies, waits for them, and re-layouts: 30.4 us -> none  [the longest x1 15.3 us: per_device(): send_state = jnp.zeros((groups * capacity,) + old_state.shape[1:], jnp.bf...]
    all_to_all x3 -> x0, waiting for transfers between devices: 20 us -> none  [the longest x1 13.3 us: per_device(): lax.all_to_all(send_state, 'group', split_axis=0, concat_axis=0, tiled=True)]
    ppermute x6 -> x0, starting transfers between devices: 19.7 us -> none  [the longest x3 15.9 us: with_halo(): lax.ppermute(lax.slice_in_dim(block, block.shape[dim] - width, None, axis...]
  transfers between devices with their start and end apart: 9 -> 0, of which waited for: 2 -> 0; matrix products, arithmetic and copies ran while one was open for 26% -> 0% of each run, Pallas kernels for 0% -> 0%
where the time goes in v1:
time: 80.3 us; the launch traced here: 79.7 us
  Pallas kernels  74.8 us (93%)
  local copies, waits for them, and re-layouts  4.91 us (6%)
    pallas_call x1, Pallas kernels, per_device(): pl.pallas_call(functools.partial(kernel, across, along, members, per), ou...  74.8 us
    unnamed x10, local copies, waits for them, and re-layouts  4.91 us

profile of v1, /device:TPU:6, one launch (start us, length us, event | category | flops | bytes accessed | tf_op | source)
XLA Modules:
  0.0 79.7 jit_solution(4255229039806822598)
XLA Ops:
  0.0 0.7 copy.8
  0.7 0.0 copy-start
  0.7 1.1 %copy-done = bf16[1,1,128,9,256]{4,2,3,1,0:T(8,128)(2,1)S(1)} copy-done((bf16[1,1,128,9,256]{4,2,3,1,0:T(8,128)(2,1)S(1)}, bf16[1,1,128,9,256]{4,2,3,1,0:T(8,128)(2,1)}, u32[]{:S(2)}) %copy-start) | copy-done | bytes 589848
  1.8 0.0 copy-start.1
  1.8 0.8 %copy-done.1 = bf16[1,1,128,256]{3,2,1,0:T(8,128)(2,1)S(1)} copy-done((bf16[1,1,128,256]{3,2,1,0:T(8,128)(2,1)S(1)}, bf16[1,1,128,256]{3,2,1,0:T(8,128)(2,1)}, u32[]{:S(2)}) %copy-start.1) | copy-done | bytes 65560
  2.6 0.0 copy-start.2
  2.6 0.7 copy-done.2
  3.2 0.0 copy-start.3
  3.2 0.7 copy-done.3
  3.9 74.8 %regrid_and_sweep.1 = f32[9,128,256]{2,1,0:T(8,128)S(1)} custom-call(s32[1,128]{1,0:T(1,128)S(1)} %bitcast.15, s32[6,128]{1,0:T(8,128)S(1)} %bitcast.14, f32[9]{0:T(128)S(1)} %copy-done.3, bf16[128,256]{1,0:T(8,128)(2,1)S(1)} %bitcast.13, bf16[9,128,256]{2,1,0:T(8,128)(2,1)S(1)} %bitcast.12), custom_call_target="tpu_custom_call" | custom-call | tf_op jit(solution)/shard_map/regrid_and_sweep/pallas_call | solution.py:299
  78.7 1.0 %copy.10 = f32[1,1,128,9,256]{4,2,3,1,0:T(8,128)} copy(f32[1,1,128,9,256]{4,2,3,1,0:T(8,128)S(1)} %bitcast.11) | data formatting | bytes 2359296
Async XLA Ops:
  0.7 1.1 %copy-start = (bf16[1,1,128,9,256]{4,2,3,1,0:T(8,128)(2,1)S(1)}, bf16[1,1,128,9,256]{4,2,3,1,0:T(8,128)(2,1)}, u32[]{:S(2)}) copy-start(bf16[1,1,128,9,256]{4,2,3,1,0:T(8,128)(2,1)} %param.5) | copy-start | bytes 1769476
  1.8 0.8 %copy-start.1 = (bf16[1,1,128,256]{3,2,1,0:T(8,128)(2,1)S(1)}, bf16[1,1,128,256]{3,2,1,0:T(8,128)(2,1)}, u32[]{:S(2)}) copy-start(bf16[1,1,128,256]{3,2,1,0:T(8,128)(2,1)} %param.6) | copy-start | bytes 196612
  2.6 0.7 copy-start.2
  3.2 0.7 copy-start.3

commit v2 on v1

v2 whole, which is shorter than its diff:
```python
import functools
import math

import jax
import jax.numpy as jnp
from jax import lax
from jax.experimental import pallas as pl
from jax.experimental.pallas import tpu as pltpu
from jax.sharding import PartitionSpec as P

LANES = 128
EDGE = 16
PER = 2
GROUP = 3
AHEAD = 3
BEHIND = 2
TOP = 32767.0
MESH = pl.DeviceIdType.MESH
F32 = jnp.float32
BF16 = jnp.bfloat16


def dot(left, right):
    return jnp.dot(left, right, preferred_element_type=F32)


def iota(shape, dim):
    return lax.broadcasted_iota(jnp.int32, shape, dim)


def ones_where(mask):
    return jnp.where(mask, 1.0, 0.0).astype(BF16)


def beside(field, picked):
    rows = field.shape[0]
    low, high = field[:, :LANES], field[:, LANES:]
    lane = iota((rows, LANES), 1)
    xpos = lane % EDGE

    def turn(part, by):
        return pltpu.roll(part, by % LANES, 1)

    def halves(part):
        return part[:, :LANES], part[:, LANES:]

    def both(one, two):
        return jnp.concatenate([one, two], axis=1)

    a, b = halves(picked[0])
    x_low = both(
        jnp.where(xpos == 0, turn(a, 1 - EDGE), turn(low, 1)),
        jnp.where(xpos == 0, turn(b, 1 - EDGE), turn(high, 1)),
    )
    a, b = halves(picked[1])
    x_high = both(
        jnp.where(xpos == EDGE - 1, turn(a, EDGE - 1), turn(low, -1)),
        jnp.where(xpos == EDGE - 1, turn(b, EDGE - 1), turn(high, -1)),
    )
    first = lane < EDGE
    low_up, high_up = turn(low, EDGE), turn(high, EDGE)
    y_low = both(
        jnp.where(first, turn(picked[2][:, LANES:], EDGE), low_up),
        jnp.where(first, low_up, high_up),
    )
    last = lane >= LANES - EDGE
    low_down, high_down = turn(low, -EDGE), turn(high, -EDGE)
    y_high = both(
        jnp.where(last, high_down, low_down),
        jnp.where(last, turn(picked[3][:, :LANES], -EDGE), high_down),
    )
    return x_low, x_high, y_low, y_high


def split(value):
    head = value.astype(BF16)
    return head, (value - head.astype(F32)).astype(BF16)


def kernel(
    across, along, members, per,
    dest_hbm, lists_hbm, lewis_hbm, coef_hbm, state_hbm, out_ref,
    dest_ref, lists_ref, lewis_ref, coef_ref, state_ref,
    send1, recv1, send2, arrived, below, above, kept, weight, total, pick1, pick2,
    code, code_low, code_high, scale, scale_low, scale_high,
    s0, s1, r1, s2, r2, sz, rz, sp, rp, sq, rq,
):
    species, slots, cells = state_ref.shape
    groups = species // GROUP
    chunks = (species + 1) // per
    group, member = lax.axis_index("group"), lax.axis_index("member")
    yme, xme = group // across, group % across
    has_upper, has_lower = member < members - 1, member > 0
    upper, lower = jnp.where(has_upper, member + 1, member - 1), jnp.where(has_lower, member - 1, member + 1)
    xrows, yrows = 2 * along, 2 * across

    xpeers = [lax.rem(xme + step, across) for step in range(1, across)]
    ypeers = [lax.rem(yme + step, along) for step in range(1, along)]
    xdevices = [yme * across + peer for peer in xpeers]
    ydevices = [peer * across + xme for peer in ypeers]

    barrier = pltpu.get_barrier_semaphore()
    for device in xdevices + ydevices:
        pl.semaphore_signal(barrier, inc=1, device_id=(device, member), device_id_type=MESH)

    @pl.when(has_upper)
    def _():
        pl.semaphore_signal(barrier, inc=1, device_id=(group, upper), device_id_type=MESH)

    @pl.when(has_lower)
    def _():
        pl.semaphore_signal(barrier, inc=1, device_id=(group, lower), device_id_type=MESH)

    loads = [
        pltpu.make_async_copy(here, there, s0.at[i])
        for i, (here, there) in enumerate((
            (dest_hbm, dest_ref), (coef_hbm, coef_ref), (state_hbm, state_ref),
            (lists_hbm, lists_ref), (lewis_hbm, lewis_ref),
        ))
    ]
    for load in loads:
        load.start()

    @pl.when(jnp.logical_not(has_lower))
    def _():
        below[...] = jnp.zeros_like(below)
        scale_low[...] = jnp.zeros_like(scale_low)
        code_low[...] = jnp.zeros_like(code_low)

    @pl.when(jnp.logical_not(has_upper))
    def _():
        above[...] = jnp.zeros_like(above)
        scale_high[...] = jnp.zeros_like(scale_high)
        code_high[...] = jnp.zeros_like(code_high)

    row = iota((slots, slots), 0)
    col = iota((slots, slots), 1)
    earlier = ones_where(row < col)

    target = (row % xrows) // 2 * across + row // xrows
    loads[0].wait()
    match = ones_where(dest_ref[...] == target)
    rank = dot(match, earlier).astype(jnp.int32)
    chosen = ones_where((match > 0) & (rank == row % 2))
    source = (row % yrows) // 2 * xrows + row // yrows * 2 + row % 2
    swap = ones_where(source == col)

    def blocks(peers, size):
        return [pl.ds(pl.multiple_of(peer * size, size), size) for peer in peers]

    xblocks, yblocks = blocks(xpeers, xrows), blocks(ypeers, yrows)
    (xmine,), (ymine,) = blocks([xme], xrows), blocks([yme], yrows)

    def send(chunk, here, there, mine, targets, sends, gets):
        part = pl.ds(chunk * per, per)
        for rows, device in targets:
            pltpu.make_async_remote_copy(
                src_ref=here.at[part, rows], dst_ref=there.at[part, mine],
                send_sem=sends.at[chunk], recv_sem=gets.at[chunk],
                device_id=(device, member), device_id_type=MESH,
            ).start()

    def wait(chunk, place, size, semaphores):
        others = place.at[pl.ds(chunk * per, per), pl.ds(0, slots - size)]
        pltpu.make_async_copy(others, others, semaphores.at[chunk]).wait()

    def zcopies(chunk):
        part = pl.ds(chunk * per, per)
        return [
            (arrived.at[part], place.at[part], sz.at[chunk, way], rz.at[chunk, way], way)
            for way, place in enumerate((below, above))
        ]

    def gcopies(part):
        return [
            (here.at[span], place.at[span], sends.at[part, way], gets.at[part, way], way)
            for here, places, sends, gets, span in (
                (code, (code_low, code_high), sp, rp, pl.ds(part * GROUP, GROUP)),
                (scale, (scale_low, scale_high), sq, rq, part),
            )
            for way, place in enumerate(places)
        ]

    def along_z(copies, act):
        for here, place, send, get, way in copies:
            copy = pltpu.make_async_remote_copy(
                src_ref=here, dst_ref=place, send_sem=send, recv_sem=get,
                device_id=(group, lower if way else upper), device_id_type=MESH,
            )
            there = has_lower if (act == "wait_recv") != (way == 1) else has_upper
            pl.when(there)(getattr(copy, act))

    def pack(chunk, first):
        for j in range(per):
            plane = chunk * per + j
            block = coef_ref[...] if first and j == 0 else state_ref[plane - 1]
            send1[plane] = dot(chosen, block).astype(BF16)
        part = pl.ds(chunk * per, per)
        recv1[part, xmine, :] = send1[part, xmine, :]

    def spread(chunk):
        send(chunk, send1, recv1, xmine, list(zip(xblocks, xdevices)), s1, r1)

    def turn(chunk):
        wait(chunk, recv1, xrows, r1)
        for j in range(per):
            plane = chunk * per + j
            send2[plane] = dot(swap, recv1[plane]).astype(BF16)
        send(chunk, send2, arrived, ymine, list(zip(yblocks, ydevices)), s2, r2)
        part = pl.ds(chunk * per, per)
        arrived[part, ymine, :] = send2[part, ymine, :]

    def forward(chunk):
        wait(chunk, arrived, yrows, r2)
        along_z(zcopies(chunk), "start")

    loads[1].wait()
    loads[2].wait()
    pack(0, True)
    loads[3].wait()
    loads[4].wait()
    for face in range(6):
        pick2[face] = jnp.where(lists_ref[face] == row, 1.0, 0.0).T.astype(BF16)
    pl.semaphore_wait(
        barrier, across + along - 2 + has_upper.astype(jnp.int32) + has_lower.astype(jnp.int32)
    )
    spread(0)

    def placing(field):
        lead = ones_where(iota((8, cells), 1) == 0)
        value = lax.dot_general(lead, field, (((1,), (1,)), ((), ())), preferred_element_type=F32)
        there = ones_where(value > 0.25)
        place = dot(there, earlier)[0:1].astype(jnp.int32)
        return ones_where((place == row) & (there[0:1] > 0))

    def first_near(plane):
        block = arrived[plane]
        field = dot(pick1[0], block)
        near = beside(field, [dot(pick1[face + 1], block) for face in range(4)])
        return field, near + (dot(pick1[5], below[plane]), dot(pick1[6], above[plane]))

    def setup():
        order = placing(arrived[0])
        pick1[0] = order
        for face in range(4):
            pick1[face + 1] = dot(pick2[face], order).astype(BF16)
        pick1[5] = dot(pick2[4], placing(below[0])).astype(BF16)
        pick1[6] = dot(pick2[5], placing(above[0])).astype(BF16)

        field, near = first_near(0)
        summed = None
        for face in range(6):
            part = 0.5 * (field + near[face])
            weight[face] = part
            summed = part if summed is None else summed + part
        total[...] = summed

    def relax(kind, rhs, near):
        flow = weight[0] * near[0]
        for face in range(1, 6):
            flow = flow + weight[face] * near[face]
        factor = lewis_ref[kind]
        return (rhs + factor * flow) / (1.0 + factor * total[...])

    def relax_first(plane):
        kind = plane - 1
        rhs, near = first_near(plane)
        kept[kind] = rhs.astype(BF16)
        phi = relax(kind, rhs, near)
        out_ref[kind] = phi
        largest = jnp.maximum(jnp.max(jnp.abs(phi), axis=1, keepdims=True), 1e-30)
        unit = (largest * (1.01 / TOP)).astype(BF16).astype(F32)
        code[kind] = jnp.round(phi * (1.0 / unit)).astype(jnp.int32).astype(jnp.int16)
        part = kind // GROUP
        across_lanes = dot(jnp.ones((16, slots), BF16), jnp.where(row == col, unit, 0.0).astype(BF16))
        scale[part, pl.ds(kind % GROUP, 1), :] = across_lanes[:1]

        @pl.when(kind % GROUP == GROUP - 1)
        def _():
            along_z(gcopies(part), "start")

    @pl.loop(1, chunks + AHEAD + 1 + BEHIND)
    def _(step):
        @pl.when(step < chunks)
        def _():
            pack(step, False)
            spread(step)

        @pl.when((step >= AHEAD) & (step < chunks + AHEAD))
        def _():
            turn(step - AHEAD)

        @pl.when((step >= AHEAD + 1) & (step < chunks + AHEAD + 1))
        def _():
            forward(step - AHEAD - 1)

        @pl.when(step >= AHEAD + 1 + BEHIND)
        def _():
            chunk = step - AHEAD - 1 - BEHIND
            along_z(zcopies(chunk), "wait_recv")
            pl.when(chunk == 0)(setup)
            pl.loop(jnp.where(chunk == 0, 1, chunk * per), chunk * per + per)(relax_first)

    @pl.loop(0, chunks)
    def _(chunk):
        wait(chunk, send1, xrows, s1)
        wait(chunk, send2, yrows, s2)
        along_z(zcopies(chunk), "wait_send")

    @pl.loop(0, species)
    def _(kind):
        phi = out_ref[kind]
        head, tail = split(phi)
        pair = jnp.concatenate([head, tail], axis=0)
        near = beside(
            phi, [dot(jnp.concatenate([pick2[face], pick2[face]], axis=1), pair) for face in range(4)]
        )
        part = kind // GROUP

        @pl.when(kind % GROUP == 0)
        def _():
            along_z(gcopies(part), "wait_recv")

        ends = ()
        for face, codes, scales in ((4, code_low, scale_low), (5, code_high, scale_high)):
            value = codes[kind].astype(jnp.int32).astype(F32)
            high = jnp.floor(value * (1.0 / 256.0) + 0.5)
            pair = jnp.concatenate([high.astype(BF16), (value - 256.0 * high).astype(BF16)], axis=0)
            hot = pick2[face].astype(F32) * scales[part, pl.ds(kind % GROUP, 1), :]
            ends += (dot(jnp.concatenate([(256.0 * hot).astype(BF16), hot.astype(BF16)], axis=1), pair),)
        out_ref[kind] = relax(kind, kept[kind].astype(F32), near + ends)

    @pl.loop(0, groups)
    def _(part):
        along_z(gcopies(part), "wait_send")


def per_device(across, along, members, state, coef, new_group, face_lists, lewis):
    _, _, slots, species, cells = state.shape
    per = PER
    chunks = (species + 1) // per
    whole = pl.BlockSpec(memory_space=pltpu.VMEM)
    far = pl.BlockSpec(memory_space=pltpu.HBM)
    groups = species // GROUP
    dma = pltpu.SemaphoreType.DMA
    planes = (species + 1, slots, cells)
    out = pl.pallas_call(
        functools.partial(kernel, across, along, members, per),
        out_shape=jax.ShapeDtypeStruct((species, slots, cells), F32),
        in_specs=[far] * 5,
        out_specs=whole,
        scratch_shapes=[
            pltpu.VMEM((1, slots), jnp.int32),
            pltpu.VMEM((6, 1, slots), jnp.int32),
            pltpu.SMEM((species,), F32),
            pltpu.VMEM((slots, cells), BF16),
            pltpu.VMEM((species, slots, cells), BF16),
            pltpu.VMEM(planes, BF16),
            pltpu.VMEM(planes, BF16),
            pltpu.VMEM(planes, BF16),
            pltpu.VMEM(planes, BF16),
            pltpu.VMEM(planes, BF16),
            pltpu.VMEM(planes, BF16),
            pltpu.VMEM((species, slots, cells), BF16),
            pltpu.VMEM((6, slots, cells), F32),
            pltpu.VMEM((slots, cells), F32),
            pltpu.VMEM((7, slots, slots), BF16),
            pltpu.VMEM((6, slots, slots), BF16),
            pltpu.VMEM((species, slots, cells), jnp.int16),
            pltpu.VMEM((species, slots, cells), jnp.int16),
            pltpu.VMEM((species, slots, cells), jnp.int16),
            pltpu.VMEM((groups, 8, slots), F32),
            pltpu.VMEM((groups, 8, slots), F32),
            pltpu.VMEM((groups, 8, slots), F32),
            dma((5,)),
            dma((chunks,)),
            dma((chunks,)),
            dma((chunks,)),
            dma((chunks,)),
            dma((chunks, 2)),
            dma((chunks, 2)),
            dma((groups, 2)),
            dma((groups, 2)),
            dma((groups, 2)),
            dma((groups, 2)),
        ],
        compiler_params=pltpu.CompilerParams(
            collective_id=0, has_side_effects=True, vmem_limit_bytes=60 * 2**20
        ),
        name="regrid_and_sweep",
    )(
        new_group[0],
        jnp.transpose(face_lists[0], (1, 0, 2)),
        lewis,
        coef[0, 0],
        jnp.transpose(state[0, 0], (1, 0, 2)),
    )
    return jnp.transpose(out, (1, 0, 2))[None, None]


def solution(mesh):
    groups, members = mesh.shape["group"], mesh.shape["member"]
    across = math.isqrt(groups)
    return jax.shard_map(
        functools.partial(per_device, across, groups // across, members),
        mesh=mesh,
        in_specs=(
            P("group", "member", None, None, None),
            P("group", "member", None, None),
            P("group", "member", None),
            P("group", "member", None, None),
            P(),
        ),
        out_specs=P("group", "member", None, None, None),
        check_vma=False,
    )
```

time: 80.3 us -> 57 us (0.71)
  Pallas kernels: 74.8 us -> 53.5 us
  local copies, waits for them, and re-layouts: 4.91 us -> 2.36 us
    pallas_call x1, Pallas kernels: 74.8 us -> 53.5 us  [per_device(): pl.pallas_call(functools.partial(kernel, across, along, members, per), ou...]
    unnamed x10 -> x1, local copies, waits for them, and re-layouts: 4.91 us -> 2.36 us
where the time goes in v2:
time: 57 us; the launch traced here: 55.9 us
  Pallas kernels  53.5 us (94%)
  local copies, waits for them, and re-layouts  2.36 us (4%)
    pallas_call x1, Pallas kernels, per_device(): pl.pallas_call(functools.partial(kernel, across, along, members, per), ou...  53.5 us
    unnamed x1, local copies, waits for them, and re-layouts  2.36 us

profile of v2, /device:TPU:6, one launch (start us, length us, event | category | flops | bytes accessed | tf_op | source)
XLA Modules:
  0.0 55.9 jit_solution(7569087347850242530)
XLA Ops:
  0.0 53.5 %regrid_and_sweep.1 = f32[9,128,256]{2,1,0:T(8,128)} custom-call(s32[1,128]{1,0:T(1,128)} %bitcast.13, s32[6,1,128]{2,1,0:T(1,128)} %bitcast.12, f32[9]{0:T(128)} %lewis_hbm.1, bf16[128,256]{1,0:T(8,128)(2,1)} %bitcast.11, bf16[9,128,256]{2,1,0:T(8,128)(2,1)} %bitcast.10), custom_call_target="tpu_custom_call" | custom-call | tf_op jit(solution)/shard_map/regrid_and_sweep/pallas_call | solution.py:347
  53.5 2.4 %copy.7 = f32[1,1,128,9,256]{4,2,3,1,0:T(8,128)} copy(f32[1,1,128,9,256]{4,2,3,1,0:T(8,128)} %bitcast.9) | data formatting | bytes 2359296

commit v3 on v2

--- a/solution.py
+++ b/solution.py
@@ -10,9 +10,10 @@
 
 LANES = 128
 EDGE = 16
-PER = 2
+SIZES = (1, 2, 2, 2, 3)
 GROUP = 3
-AHEAD = 3
+AHEAD = 2
+LAG = 1
 BEHIND = 2
 TOP = 32767.0
 MESH = pl.DeviceIdType.MESH
@@ -78,7 +79,7 @@
 
 
 def kernel(
-    across, along, members, per,
+    across, along, members, sizes,
     dest_hbm, lists_hbm, lewis_hbm, coef_hbm, state_hbm, out_ref,
     dest_ref, lists_ref, lewis_ref, coef_ref, state_ref,
     send1, recv1, send2, arrived, below, above, kept, weight, total, pick1, pick2,
@@ -87,7 +88,8 @@
 ):
     species, slots, cells = state_ref.shape
     groups = species // GROUP
-    chunks = (species + 1) // per
+    chunks = len(sizes)
+    parts = [pl.ds(sum(sizes[:chunk]), sizes[chunk]) for chunk in range(chunks)]
     group, member = lax.axis_index("group"), lax.axis_index("member")
     yme, xme = group // across, group % across
     has_upper, has_lower = member < members - 1, member > 0
@@ -98,18 +100,6 @@
     ypeers = [lax.rem(yme + step, along) for step in range(1, along)]
     xdevices = [yme * across + peer for peer in xpeers]
     ydevices = [peer * across + xme for peer in ypeers]
-
-    barrier = pltpu.get_barrier_semaphore()
-    for device in xdevices + ydevices:
-        pl.semaphore_signal(barrier, inc=1, device_id=(device, member), device_id_type=MESH)
-
-    @pl.when(has_upper)
-    def _():
-        pl.semaphore_signal(barrier, inc=1, device_id=(group, upper), device_id_type=MESH)
-
-    @pl.when(has_lower)
-    def _():
-        pl.semaphore_signal(barrier, inc=1, device_id=(group, lower), device_id_type=MESH)
 
     loads = [
         pltpu.make_async_copy(here, there, s0.at[i])
@@ -121,17 +111,17 @@
     for load in loads:
         load.start()
 
-    @pl.when(jnp.logical_not(has_lower))
+    barrier = pltpu.get_barrier_semaphore()
+    for device in xdevices + ydevices:
+        pl.semaphore_signal(barrier, inc=1, device_id=(device, member), device_id_type=MESH)
+
+    @pl.when(has_upper)
     def _():
-        below[...] = jnp.zeros_like(below)
-        scale_low[...] = jnp.zeros_like(scale_low)
-        code_low[...] = jnp.zeros_like(code_low)
-
-    @pl.when(jnp.logical_not(has_upper))
+        pl.semaphore_signal(barrier, inc=1, device_id=(group, upper), device_id_type=MESH)
+
+    @pl.when(has_lower)
     def _():
-        above[...] = jnp.zeros_like(above)
-        scale_high[...] = jnp.zeros_like(scale_high)
-        code_high[...] = jnp.zeros_like(code_high)
+        pl.semaphore_signal(barrier, inc=1, device_id=(group, lower), device_id_type=MESH)
 
     row = iota((slots, slots), 0)
     col = iota((slots, slots), 1)
@@ -152,7 +142,7 @@
     (xmine,), (ymine,) = blocks([xme], xrows), blocks([yme], yrows)
 
     def send(chunk, here, there, mine, targets, sends, gets):
-        part = pl.ds(chunk * per, per)
+        part = parts[chunk]
         for rows, device in targets:
             pltpu.make_async_remote_copy(
                 src_ref=here.at[part, rows], dst_ref=there.at[part, mine],
@@ -161,11 +151,11 @@
             ).start()
 
     def wait(chunk, place, size, semaphores):
-        others = place.at[pl.ds(chunk * per, per), pl.ds(0, slots - size)]
+        others = place.at[parts[chunk], pl.ds(0, slots - size)]
         pltpu.make_async_copy(others, others, semaphores.at[chunk]).wait()
 
     def zcopies(chunk):
-        part = pl.ds(chunk * per, per)
+        part = parts[chunk]
         return [
             (arrived.at[part], place.at[part], sz.at[chunk, way], rz.at[chunk, way], way)
             for way, place in enumerate((below, above))
@@ -190,12 +180,11 @@
             there = has_lower if (act == "wait_recv") != (way == 1) else has_upper
             pl.when(there)(getattr(copy, act))
 
-    def pack(chunk, first):
-        for j in range(per):
-            plane = chunk * per + j
-            block = coef_ref[...] if first and j == 0 else state_ref[plane - 1]
+    def pack(chunk):
+        for plane in range(parts[chunk].start, parts[chunk].start + parts[chunk].size):
+            block = state_ref[plane - 1] if plane else coef_ref[...]
             send1[plane] = dot(chosen, block).astype(BF16)
-        part = pl.ds(chunk * per, per)
+        part = parts[chunk]
         recv1[part, xmine, :] = send1[part, xmine, :]
 
     def spread(chunk):
@@ -203,28 +192,45 @@
 
     def turn(chunk):
         wait(chunk, recv1, xrows, r1)
-        for j in range(per):
-            plane = chunk * per + j
+        for plane in range(parts[chunk].start, parts[chunk].start + parts[chunk].size):
             send2[plane] = dot(swap, recv1[plane]).astype(BF16)
         send(chunk, send2, arrived, ymine, list(zip(yblocks, ydevices)), s2, r2)
-        part = pl.ds(chunk * per, per)
+        part = parts[chunk]
         arrived[part, ymine, :] = send2[part, ymine, :]
 
     def forward(chunk):
         wait(chunk, arrived, yrows, r2)
         along_z(zcopies(chunk), "start")
 
+    def start(chunk):
+        pack(chunk)
+        spread(chunk)
+
     loads[1].wait()
+    pack(0)
+    pl.semaphore_wait(
+        barrier, across + along - 2 + has_upper.astype(jnp.int32) + has_lower.astype(jnp.int32)
+    )
+    spread(0)
     loads[2].wait()
-    pack(0, True)
+    start(1)
+
     loads[3].wait()
     loads[4].wait()
     for face in range(6):
         pick2[face] = jnp.where(lists_ref[face] == row, 1.0, 0.0).T.astype(BF16)
-    pl.semaphore_wait(
-        barrier, across + along - 2 + has_upper.astype(jnp.int32) + has_lower.astype(jnp.int32)
-    )
-    spread(0)
+
+    @pl.when(jnp.logical_not(has_lower))
+    def _():
+        below[...] = jnp.zeros_like(below)
+        scale_low[...] = jnp.zeros_like(scale_low)
+        code_low[...] = jnp.zeros_like(code_low)
+
+    @pl.when(jnp.logical_not(has_upper))
+    def _():
+        above[...] = jnp.zeros_like(above)
+        scale_high[...] = jnp.zeros_like(scale_high)
+        code_high[...] = jnp.zeros_like(code_high)
 
     def placing(field):
         lead = ones_where(iota((8, cells), 1) == 0)
@@ -255,18 +261,20 @@
             summed = part if summed is None else summed + part
         total[...] = summed
 
-    def relax(kind, rhs, near):
-        flow = weight[0] * near[0]
-        for face in range(1, 6):
-            flow = flow + weight[face] * near[face]
+    def relax(kind, rhs, near, faces):
+        flow = None
+        for face, value in zip(faces, near):
+            part = weight[face] * value
+            flow = part if flow is None else flow + part
         factor = lewis_ref[kind]
-        return (rhs + factor * flow) / (1.0 + factor * total[...])
+        share = 1.0 / (1.0 + factor * total[...])
+        return rhs * share + (factor * share) * flow if rhs is not None else (factor * share) * flow
 
     def relax_first(plane):
         kind = plane - 1
         rhs, near = first_near(plane)
         kept[kind] = rhs.astype(BF16)
-        phi = relax(kind, rhs, near)
+        phi = relax(kind, rhs, near, range(6))
         out_ref[kind] = phi
         largest = jnp.maximum(jnp.max(jnp.abs(phi), axis=1, keepdims=True), 1e-30)
         unit = (largest * (1.01 / TOP)).astype(BF16).astype(F32)
@@ -279,30 +287,25 @@
         def _():
             along_z(gcopies(part), "start")
 
-    @pl.loop(1, chunks + AHEAD + 1 + BEHIND)
-    def _(step):
-        @pl.when(step < chunks)
-        def _():
-            pack(step, False)
-            spread(step)
-
-        @pl.when((step >= AHEAD) & (step < chunks + AHEAD))
-        def _():
+    def sweep(chunk):
+        along_z(zcopies(chunk), "wait_recv")
+        if chunk == 0:
+            setup()
+        first = parts[chunk].start
+        pl.loop(max(first, 1), first + parts[chunk].size)(relax_first)
+
+    for step in range(2, chunks + AHEAD + LAG + BEHIND):
+        if step < chunks:
+            start(step)
+        if 0 <= step - AHEAD < chunks:
             turn(step - AHEAD)
-
-        @pl.when((step >= AHEAD + 1) & (step < chunks + AHEAD + 1))
-        def _():
-            forward(step - AHEAD - 1)
-
-        @pl.when(step >= AHEAD + 1 + BEHIND)
-        def _():
-            chunk = step - AHEAD - 1 - BEHIND
-            along_z(zcopies(chunk), "wait_recv")
-            pl.when(chunk == 0)(setup)
-            pl.loop(jnp.where(chunk == 0, 1, chunk * per), chunk * per + per)(relax_first)
-
-    @pl.loop(0, chunks)
-    def _(chunk):
+        if 0 <= step - AHEAD - LAG < chunks:
+            forward(step - AHEAD - LAG)
+        chunk = step - AHEAD - LAG - BEHIND
+        if 0 <= chunk < chunks:
+            sweep(chunk)
+
+    for chunk in range(chunks):
         wait(chunk, send1, xrows, s1)
         wait(chunk, send2, yrows, s2)
         along_z(zcopies(chunk), "wait_send")
@@ -315,6 +318,10 @@
         near = beside(
             phi, [dot(jnp.concatenate([pick2[face], pick2[face]], axis=1), pair) for face in range(4)]
         )
+        out_ref[kind] = relax(kind, kept[kind].astype(F32), near, range(4))
+
+    @pl.loop(0, species)
+    def _(kind):
         part = kind // GROUP
 
         @pl.when(kind % GROUP == 0)
@@ -328,7 +335,7 @@
             pair = jnp.concatenate([high.astype(BF16), (value - 256.0 * high).astype(BF16)], axis=0)
             hot = pick2[face].astype(F32) * scales[part, pl.ds(kind % GROUP, 1), :]
             ends += (dot(jnp.concatenate([(256.0 * hot).astype(BF16), hot.astype(BF16)], axis=1), pair),)
-        out_ref[kind] = relax(kind, kept[kind].astype(F32), near + ends)
+        out_ref[kind] = out_ref[kind] + relax(kind, None, ends, (4, 5))
 
     @pl.loop(0, groups)
     def _(part):
@@ -337,16 +344,15 @@
 
 def per_device(across, along, members, state, coef, new_group, face_lists, lewis):
     _, _, slots, species, cells = state.shape
-    per = PER
-    chunks = (species + 1) // per
+    chunks = len(SIZES)
     whole = pl.BlockSpec(memory_space=pltpu.VMEM)
     far = pl.BlockSpec(memory_space=pltpu.HBM)
     groups = species // GROUP
     dma = pltpu.SemaphoreType.DMA
     planes = (species + 1, slots, cells)
     out = pl.pallas_call(
-        functools.partial(kernel, across, along, members, per),
-        out_shape=jax.ShapeDtypeStruct((species, slots, cells), F32),
+        functools.partial(kernel, across, along, members, SIZES),
+        out_shape=pltpu.VMEM((species, slots, cells), F32),
         in_specs=[far] * 5,
         out_specs=whole,
         scratch_shapes=[

time: 57 us -> 53.6 us (0.940)
  Pallas kernels: 53.5 us -> 51.7 us
  local copies, waits for them, and re-layouts: 2.36 us -> 1.02 us
    pallas_call x1, Pallas kernels: 53.5 us -> 51.7 us  [per_device(): pl.pallas_call(functools.partial(kernel, across, along, members, SIZES),...]
    unnamed x1, local copies, waits for them, and re-layouts: 2.36 us -> 1.02 us
where the time goes in v3:
time: 53.6 us; the launch traced here: 52.7 us
  Pallas kernels  51.7 us (96%)
  local copies, waits for them, and re-layouts  1.02 us (2%)
    pallas_call x1, Pallas kernels, per_device(): pl.pallas_call(functools.partial(kernel, across, along, members, SIZES),...  51.7 us

profile of v3, /device:TPU:6, one launch (start us, length us, event | category | flops | bytes accessed | tf_op | source)
XLA Modules:
  0.0 52.7 jit_solution(3213200937995356606)
XLA Ops:
  0.0 51.7 %regrid_and_sweep.1 = f32[9,128,256]{2,1,0:T(8,128)S(1)} custom-call(s32[1,128]{1,0:T(1,128)} %bitcast.13, s32[6,1,128]{2,1,0:T(1,128)} %bitcast.12, f32[9]{0:T(128)} %lewis_hbm.1, bf16[128,256]{1,0:T(8,128)(2,1)} %bitcast.11, bf16[9,128,256]{2,1,0:T(8,128)(2,1)} %bitcast.10), custom_call_target="tpu_custom_call" | custom-call | tf_op jit(solution)/shard_map/regrid_and_sweep/pallas_call | solution.py:353
  51.7 1.0 %copy.7 = f32[1,1,128,9,256]{4,2,3,1,0:T(8,128)} copy(f32[1,1,128,9,256]{4,2,3,1,0:T(8,128)S(1)} %bitcast.9) | data formatting | bytes 2359296

commit v4 on v3

--- a/solution.py
+++ b/solution.py
@@ -11,9 +11,7 @@
 LANES = 128
 EDGE = 16
 SIZES = (1, 2, 2, 2, 3)
-GROUP = 3
-AHEAD = 2
-LAG = 1
+EARLY = 4
 BEHIND = 2
 TOP = 32767.0
 MESH = pl.DeviceIdType.MESH
@@ -87,7 +85,6 @@
     s0, s1, r1, s2, r2, sz, rz, sp, rp, sq, rq,
 ):
     species, slots, cells = state_ref.shape
-    groups = species // GROUP
     chunks = len(sizes)
     parts = [pl.ds(sum(sizes[:chunk]), sizes[chunk]) for chunk in range(chunks)]
     group, member = lax.axis_index("group"), lax.axis_index("member")
@@ -154,6 +151,10 @@
         others = place.at[parts[chunk], pl.ds(0, slots - size)]
         pltpu.make_async_copy(others, others, semaphores.at[chunk]).wait()
 
+    def kinds(chunk):
+        first = max(parts[chunk].start, 1)
+        return pl.ds(first - 1, parts[chunk].start + parts[chunk].size - first)
+
     def zcopies(chunk):
         part = parts[chunk]
         return [
@@ -165,7 +166,7 @@
         return [
             (here.at[span], place.at[span], sends.at[part, way], gets.at[part, way], way)
             for here, places, sends, gets, span in (
-                (code, (code_low, code_high), sp, rp, pl.ds(part * GROUP, GROUP)),
+                (code, (code_low, code_high), sp, rp, kinds(part)),
                 (scale, (scale_low, scale_high), sq, rq, part),
             )
             for way, place in enumerate(places)
@@ -215,22 +216,27 @@
     loads[2].wait()
     start(1)
 
-    loads[3].wait()
-    loads[4].wait()
-    for face in range(6):
-        pick2[face] = jnp.where(lists_ref[face] == row, 1.0, 0.0).T.astype(BF16)
-
-    @pl.when(jnp.logical_not(has_lower))
-    def _():
-        below[...] = jnp.zeros_like(below)
-        scale_low[...] = jnp.zeros_like(scale_low)
-        code_low[...] = jnp.zeros_like(code_low)
-
-    @pl.when(jnp.logical_not(has_upper))
-    def _():
-        above[...] = jnp.zeros_like(above)
-        scale_high[...] = jnp.zeros_like(scale_high)
-        code_high[...] = jnp.zeros_like(code_high)
+    for chunk in range(2, 1 + EARLY):
+        start(chunk)
+    turn(0)
+
+    def prepare():
+        loads[3].wait()
+        loads[4].wait()
+        for face in range(6):
+            pick2[face] = jnp.where(lists_ref[face] == row, 1.0, 0.0).T.astype(BF16)
+
+        @pl.when(jnp.logical_not(has_lower))
+        def _():
+            below[...] = jnp.zeros_like(below)
+            scale_low[...] = jnp.zeros_like(scale_low)
+            code_low[...] = jnp.zeros_like(code_low)
+
+        @pl.when(jnp.logical_not(has_upper))
+        def _():
+            above[...] = jnp.zeros_like(above)
+            scale_high[...] = jnp.zeros_like(scale_high)
+            code_high[...] = jnp.zeros_like(code_high)
 
     def placing(field):
         lead = ones_where(iota((8, cells), 1) == 0)
@@ -270,40 +276,37 @@
         share = 1.0 / (1.0 + factor * total[...])
         return rhs * share + (factor * share) * flow if rhs is not None else (factor * share) * flow
 
-    def relax_first(plane):
-        kind = plane - 1
-        rhs, near = first_near(plane)
+    def relax_first(chunk, kind):
+        rhs, near = first_near(kind + 1)
         kept[kind] = rhs.astype(BF16)
         phi = relax(kind, rhs, near, range(6))
         out_ref[kind] = phi
         largest = jnp.maximum(jnp.max(jnp.abs(phi), axis=1, keepdims=True), 1e-30)
         unit = (largest * (1.01 / TOP)).astype(BF16).astype(F32)
         code[kind] = jnp.round(phi * (1.0 / unit)).astype(jnp.int32).astype(jnp.int16)
-        part = kind // GROUP
         across_lanes = dot(jnp.ones((16, slots), BF16), jnp.where(row == col, unit, 0.0).astype(BF16))
-        scale[part, pl.ds(kind % GROUP, 1), :] = across_lanes[:1]
-
-        @pl.when(kind % GROUP == GROUP - 1)
-        def _():
-            along_z(gcopies(part), "start")
+        scale[chunk, pl.ds(kind - kinds(chunk).start, 1), :] = across_lanes[:1]
 
     def sweep(chunk):
         along_z(zcopies(chunk), "wait_recv")
         if chunk == 0:
             setup()
-        first = parts[chunk].start
-        pl.loop(max(first, 1), first + parts[chunk].size)(relax_first)
-
-    for step in range(2, chunks + AHEAD + LAG + BEHIND):
+        part = kinds(chunk)
+        if part.size:
+            pl.loop(part.start, part.start + part.size)(functools.partial(relax_first, chunk))
+            along_z(gcopies(chunk), "start")
+
+    for step in range(1, chunks + 1 + BEHIND):
+        if step + EARLY < chunks:
+            start(step + EARLY)
         if step < chunks:
-            start(step)
-        if 0 <= step - AHEAD < chunks:
-            turn(step - AHEAD)
-        if 0 <= step - AHEAD - LAG < chunks:
-            forward(step - AHEAD - LAG)
-        chunk = step - AHEAD - LAG - BEHIND
-        if 0 <= chunk < chunks:
-            sweep(chunk)
+            turn(step)
+        if step <= chunks:
+            forward(step - 1)
+        if step == 1:
+            prepare()
+        if step > BEHIND:
+            sweep(step - 1 - BEHIND)
 
     for chunk in range(chunks):
         wait(chunk, send1, xrows, s1)
@@ -320,26 +323,23 @@
         )
         out_ref[kind] = relax(kind, kept[kind].astype(F32), near, range(4))
 
-    @pl.loop(0, species)
-    def _(kind):
-        part = kind // GROUP
-
-        @pl.when(kind % GROUP == 0)
-        def _():
-            along_z(gcopies(part), "wait_recv")
-
+    def last(chunk, kind):
         ends = ()
         for face, codes, scales in ((4, code_low, scale_low), (5, code_high, scale_high)):
             value = codes[kind].astype(jnp.int32).astype(F32)
             high = jnp.floor(value * (1.0 / 256.0) + 0.5)
             pair = jnp.concatenate([high.astype(BF16), (value - 256.0 * high).astype(BF16)], axis=0)
-            hot = pick2[face].astype(F32) * scales[part, pl.ds(kind % GROUP, 1), :]
+            hot = pick2[face].astype(F32) * scales[chunk, pl.ds(kind - kinds(chunk).start, 1), :]
             ends += (dot(jnp.concatenate([(256.0 * hot).astype(BF16), hot.astype(BF16)], axis=1), pair),)
         out_ref[kind] = out_ref[kind] + relax(kind, None, ends, (4, 5))
 
-    @pl.loop(0, groups)
-    def _(part):
-        along_z(gcopies(part), "wait_send")
+    busy = [chunk for chunk in range(chunks) if kinds(chunk).size]
+    for chunk in busy:
+        along_z(gcopies(chunk), "wait_recv")
+        part = kinds(chunk)
+        pl.loop(part.start, part.start + part.size)(functools.partial(last, chunk))
+    for chunk in busy:
+        along_z(gcopies(chunk), "wait_send")
 
 
 def per_device(across, along, members, state, coef, new_group, face_lists, lewis):
@@ -347,7 +347,6 @@
     chunks = len(SIZES)
     whole = pl.BlockSpec(memory_space=pltpu.VMEM)
     far = pl.BlockSpec(memory_space=pltpu.HBM)
-    groups = species // GROUP
     dma = pltpu.SemaphoreType.DMA
     planes = (species + 1, slots, cells)
     out = pl.pallas_call(
@@ -375,9 +374,9 @@
             pltpu.VMEM((species, slots, cells), jnp.int16),
             pltpu.VMEM((species, slots, cells), jnp.int16),
             pltpu.VMEM((species, slots, cells), jnp.int16),
-            pltpu.VMEM((groups, 8, slots), F32),
-            pltpu.VMEM((groups, 8, slots), F32),
-            pltpu.VMEM((groups, 8, slots), F32),
+            pltpu.VMEM((chunks, 8, slots), F32),
+            pltpu.VMEM((chunks, 8, slots), F32),
+            pltpu.VMEM((chunks, 8, slots), F32),
             dma((5,)),
             dma((chunks,)),
             dma((chunks,)),
@@ -385,10 +384,10 @@
             dma((chunks,)),
             dma((chunks, 2)),
             dma((chunks, 2)),
-            dma((groups, 2)),
-            dma((groups, 2)),
-            dma((groups, 2)),
-            dma((groups, 2)),
+            dma((chunks, 2)),
+            dma((chunks, 2)),
+            dma((chunks, 2)),
+            dma((chunks, 2)),
         ],
         compiler_params=pltpu.CompilerParams(
             collective_id=0, has_side_effects=True, vmem_limit_bytes=60 * 2**20

time: 53.6 us -> 53 us (0.989); the launches traced: 52.7 us -> 52.8 us
  no operation moved by 1% of the time
where the time goes in v4:
time: 53 us; the launch traced here: 52.8 us
  Pallas kernels  51.7 us (98%)
  local copies, waits for them, and re-layouts  1.02 us (2%)
    pallas_call x1, Pallas kernels, per_device(): pl.pallas_call(functools.partial(kernel, across, along, members, SIZES),...  51.7 us

profile of v4, /device:TPU:6, one launch (start us, length us, event | category | flops | bytes accessed | tf_op | source)
XLA Modules:
  0.0 52.8 jit_solution(13380434860417746605)
XLA Ops:
  0.0 51.7 %regrid_and_sweep.1 = f32[9,128,256]{2,1,0:T(8,128)S(1)} custom-call(s32[1,128]{1,0:T(1,128)} %bitcast.13, s32[6,1,128]{2,1,0:T(1,128)} %bitcast.12, f32[9]{0:T(128)} %lewis_hbm.1, bf16[128,256]{1,0:T(8,128)(2,1)} %bitcast.11, bf16[9,128,256]{2,1,0:T(8,128)(2,1)} %bitcast.10), custom_call_target="tpu_custom_call" | custom-call | tf_op jit(solution)/shard_map/regrid_and_sweep/pallas_call | solution.py:352
  51.8 1.0 %copy.7 = f32[1,1,128,9,256]{4,2,3,1,0:T(8,128)} copy(f32[1,1,128,9,256]{4,2,3,1,0:T(8,128)S(1)} %bitcast.9) | data formatting | bytes 2359296
